TPU v7x, 32 devices: a whole 2x2x4 slice. The times are simulated.
32 devices in a mesh: section: 8 (over z, x), dp: 4 (over y, core).
Axes of the slice: x: 2, y: 2, z: 4, core: 2. Of those that a mesh axis runs over, the one named last changes fastest.
Arguments:
- streams: bfloat16 [2, 8, 4, 128, 1024], P(None, 'section', 'dp'), may hold values from -45 to 45
- cotangents: bfloat16 [2, 8, 4, 128, 1024], P(None, 'section', 'dp'), may hold values from -6 to 6
- weights: bfloat16 [8, 1024, 4096], P('section'), may hold values from -0.1875 to 0.1875
- norm_gains: float32 [8, 1024], P('section'), may hold values from 0.25 to 1.75
- segment_ids: int32 [8, 4, 128], P(None, 'dp'), may hold values from 0 to 1, never falling along the last dimension, each value on 1 to 96 neighbouring positions
Outputs:
- out_streams: bfloat16 [2, 8, 4, 128, 1024], P(None, 'section', 'dp')
- out_cotangents: bfloat16 [2, 8, 4, 128, 1024], P(None, 'section', 'dp')
- weight_grads: bfloat16 [8, 1024, 4096], P('section', 'dp')
- gain_grads: float32 [8, 1024], P('section', 'dp')
Inputs may be any that keep to these rules, and one draw needn't show every extreme that they name: `segment_ids`: along each row of 128 tokens the document numbers never fall; each row is a 128-token window of packed documents, attention stays inside the window, and each document has 1 to 96 tokens in it.
All inputs are finite; a program needn't handle non-finite values.
Results may differ from a plain program's by a relative error of at most 0.018.
Values may be sent and summed in bfloat16 or wider, within the bound.
A program may use at most 128 MiB of HBM per device.

v0:
```python
from functools import partial
import math

import jax
import jax.numpy as jnp
from jax import lax
from jax.experimental import pallas as pl
from jax.experimental.pallas import tpu as pltpu
from jax.sharding import PartitionSpec as P

HEADS = 16
TICKS = 3
CORES = 2

epsilon = 1e-05
GELU_A = math.sqrt(2.0 / math.pi)
GELU_B = 0.044715
MESH = pl.DeviceIdType.MESH
f32 = jnp.float32
bf16 = jnp.bfloat16


def dot_nn(first, second):
    return lax.dot_general(first, second, (((1,), (0,)), ((), ())), preferred_element_type=f32)


def dot_nt(first, second):
    return lax.dot_general(first, second, (((1,), (1,)), ((), ())), preferred_element_type=f32)


def dot_tn(first, second):
    return lax.dot_general(first, second, (((0,), (0,)), ((), ())), preferred_element_type=f32)


def kernel(
    sections, replicas,
    streams, cotangents, weights, gain_ref, segs,
    out_streams, out_cotangents, grads, gain_grads,
    w, y1, y2, c1, c2, proj, dmix,
    right, normed, second, right_all, normed_all, second_all,
    dgain, dgain_send, dgain_all, acc, done,
    w_sem, in_sem, send_sem, recv_sem, own_sem, dp_send, dp_recv, dg_send, dg_recv, fin_send, fin_recv,
):
    s = lax.axis_index("section")
    r = lax.axis_index("dp")
    core = lax.rem(r, CORES)
    chip = r // CORES
    chips = replicas // CORES
    rows, dim = y1.shape[1:]
    part = dim // chips
    wide = right.shape[-1]
    own = dim // replicas
    head = dim // HEADS
    is_att = lax.rem(s, 2) == 0
    before = lax.rem(s + sections - 1, sections)
    before2 = lax.rem(s + sections - 2, sections)
    peers = [lax.rem(r + j, replicas) for j in range(1, replicas)]

    loads = [
        pltpu.make_async_copy(streams.at[0], y1.at[0], in_sem.at[0]),
        pltpu.make_async_copy(cotangents.at[1], c2.at[0], in_sem.at[1]),
        pltpu.make_async_copy(streams.at[1], y2.at[0], in_sem.at[2]),
        pltpu.make_async_copy(cotangents.at[0], c1.at[0], in_sem.at[3]),
    ]
    for copy in loads:
        copy.start()
    w_loads = [
        pltpu.make_async_copy(weights.at[:, pl.ds(j * dim, dim)], w.at[j], w_sem.at[j])
        for j in range(4)
    ]
    for copy in w_loads:
        copy.start()

    barrier = pltpu.get_barrier_semaphore()
    for step in (1, 2, sections - 1, sections - 2):
        pl.semaphore_signal(
            barrier, inc=1, device_id=(lax.rem(s + step, sections), r), device_id_type=MESH
        )
    for peer in peers:
        pl.semaphore_signal(barrier, inc=1, device_id=(s, peer), device_id_type=MESH)
    for copy in loads:
        copy.wait()
    pl.semaphore_wait(barrier, 4 + replicas - 1)

    def hand(src, dst, slot, kind, target):
        return pltpu.make_async_remote_copy(
            src_ref=src, dst_ref=dst.at[slot],
            send_sem=send_sem.at[kind, slot], recv_sem=recv_sem.at[kind, slot],
            device_id=(target, r), device_id_type=MESH,
        )

    hand(y1.at[0], y2, 1, 1, before).start()
    hand(c2.at[0], c1, 1, 2, before).start()
    for copy in w_loads:
        copy.wait()
    dgain[...] = jnp.zeros_like(dgain)

    def rows_of(tick, replica):
        return pl.ds(pl.multiple_of((tick * replicas + replica) * rows, rows), rows)

    def share(tick, j, kind):
        peer = peers[j]
        peer_core = lax.rem(peer, CORES)
        peer_chip = peer // CORES
        if kind == 0:
            src, dst = normed.at[tick, peer_chip], normed_all
        elif kind == 1:
            src, dst = second.at[tick, peer_chip], second_all
        else:
            src, dst = right.at[tick, peer_core], right_all
        return pltpu.make_async_remote_copy(
            src_ref=src, dst_ref=dst.at[rows_of(tick, r)],
            send_sem=dp_send.at[kind, tick, j], recv_sem=dp_recv.at[kind, tick, j],
            device_id=(s, peer), device_id_type=MESH,
        )

    def own_copy(tick, kind):
        if kind == 0:
            src, dst = normed.at[tick, chip], normed_all
        elif kind == 1:
            src, dst = second.at[tick, chip], second_all
        else:
            src, dst = right.at[tick, core], right_all
        return pltpu.make_async_copy(src, dst.at[rows_of(tick, r)], own_sem.at[kind, tick])

    def share_start(tick, kind):
        for j in reversed(range(replicas - 1)):
            share(tick, j, kind).start()
        own_copy(tick, kind).start()

    def tick_body(t, carry):
        @pl.when(t > 0)
        def _():
            hand(y1.at[0], y1, t, 0, before).wait_recv()

        stream = y1[t].astype(f32)
        scale = lax.rsqrt(jnp.mean(stream * stream, axis=-1, keepdims=True) + epsilon)
        n = (stream * scale * gain_ref[...]).astype(bf16)
        for c in range(chips):
            normed[t, c] = n[:, c * part : (c + 1) * part]
        share_start(t, 0)

        @pl.when(t > 0)
        def _():
            hand(c2.at[0], c2, t, 3, before).wait_recv()
            hand(y2.at[0], y2, t, 1, before).wait_recv()
            hand(c1.at[0], c1, t, 2, before).wait_recv()

        @pl.when(is_att)
        def _():
            for j in range(3):
                proj[:, j * dim : (j + 1) * dim] = dot_nn(n, w[j])
            dmix[...] = dot_nt(c2[t], w[3])
            right[t, 1, :, dim:] = c2[t]
            seg = segs[lax.rem(s + t, sections)].astype(f32)
            across = jnp.broadcast_to(seg, (rows, rows))
            row_id = lax.broadcasted_iota(jnp.int32, (rows, rows), 0)
            col_id = lax.broadcasted_iota(jnp.int32, (rows, rows), 1)
            one = ((across == across.T) & (col_id <= row_id)).astype(f32)
            keep = jnp.concatenate([one, one], axis=0)
            lane = lax.broadcasted_iota(jnp.int32, (rows, 2 * head), 1)
            low = lane < head

            def stacked(values):
                return jnp.concatenate(
                    [jnp.where(low, values, 0.0), jnp.where(low, 0.0, values)], axis=0
                )

            def merged(values):
                return jnp.where(low, values[:rows], values[rows:])

            def means(values):
                first = jnp.sum(jnp.where(low, values, 0.0), axis=-1, keepdims=True)
                last = jnp.sum(jnp.where(low, 0.0, values), axis=-1, keepdims=True)
                return first * (1.0 / head), last * (1.0 / head)

            def inv_rms(values):
                first, last = means(values * values)
                return jnp.where(low, lax.rsqrt(first + epsilon), lax.rsqrt(last + epsilon))

            def norm_back(grad, unit, inv):
                first, last = means(grad * unit)
                return inv * (grad - unit * jnp.where(low, first, last))

            def pair(i, carry):
                base = i * 2 * head
                at = [pl.ds(pl.multiple_of(base + j * dim, 2 * head), 2 * head) for j in range(3)]
                q, k = proj[:, at[0]], proj[:, at[1]]
                v = proj[:, at[2]].astype(bf16)
                q_inv, k_inv = inv_rms(q), inv_rms(k)
                q_unit, k_unit = q * q_inv, k * k_inv
                q_two = stacked(q_unit).astype(bf16)
                k_one = k_unit.astype(bf16)
                e = jnp.exp(dot_nt(q_two, k_one) * (1.0 / math.sqrt(head))) * keep
                soft = e * (1.0 / jnp.sum(e, axis=-1, keepdims=True))
                p = soft.astype(bf16)
                o = merged(dot_nn(p, v)).astype(bf16)
                per = part // (2 * head)
                second[t, i // per, :, pl.ds(pl.multiple_of(lax.rem(i, per) * 2 * head, 2 * head), 2 * head)] = o
                do = stacked(dmix[:, at[0]]).astype(bf16)
                dv = dot_tn(p, do)
                dp = dot_nt(do, v).astype(bf16).astype(f32)
                ds = soft * (dp - jnp.sum(dp * soft, axis=-1, keepdims=True))
                ds = (ds * (1.0 / math.sqrt(head))).astype(bf16)
                dq = merged(dot_nn(ds, k_one)).astype(bf16).astype(f32)
                dk = dot_tn(ds, q_two).astype(bf16).astype(f32)
                right[t, 0, :, at[0]] = norm_back(dq, q_unit, q_inv).astype(bf16)
                right[t, 0, :, at[1]] = norm_back(dk, k_unit, k_inv).astype(bf16)
                right[t, 1, :, at[0]] = dv.astype(bf16)
                return carry

            lax.fori_loop(0, HEADS // 2, pair, 0, unroll=2)

        @pl.when(jnp.logical_not(is_att))
        def _():
            for c in range(chips):
                second[t, c] = c2[t, :, c * part : (c + 1) * part]
            for j in range(2):
                at = pl.ds(j * dim, dim)
                proj[:, at] = dot_nn(n, w[j])
                dmix[...] = dot_nn(c2[t], w[2 + j])

                def strip(i, carry):
                    cols = pl.ds(pl.multiple_of(i * 256, 256), 256)
                    to = pl.ds(pl.multiple_of(j * dim + i * 256, 256), 256)
                    x = proj[:, to]
                    square = x * x
                    tanh = jnp.tanh(GELU_A * x * (1.0 + GELU_B * square))
                    half = 0.5 * (1.0 + tanh)
                    slope = half + 0.5 * x * (1.0 - tanh * tanh) * GELU_A * (1.0 + 3.0 * GELU_B * square)
                    right[t, 1, :, to] = (x * half).astype(bf16)
                    right[t, 0, :, to] = (slope * dmix[:, cols]).astype(bf16)
                    return carry

                lax.fori_loop(0, dim // 256, strip, 0)

        share_start(t, 2)
        share_start(t, 1)

        @pl.when(is_att)
        def _():
            branch = dot_nn(second[t, 0], w[3, :part])
            for c in range(1, chips):
                branch = branch + dot_nn(second[t, c], w[3, c * part : (c + 1) * part])
            y1[t + 1 + TICKS] = (y2[t].astype(f32) - branch).astype(bf16)

        @pl.when(jnp.logical_not(is_att))
        def _():
            branch = dot_nt(right[t, 1, :, :dim], w[2]) + dot_nt(right[t, 1, :, dim:], w[3])
            y1[t + 1 + TICKS] = (y2[t].astype(f32) - branch).astype(bf16)

        made, cot = t + 1 + TICKS, t + 1 + TICKS
        hand(y1.at[made], y1, t + 1, 0, before).start()

        @pl.when(is_att)
        def _():
            dmix[...] = (
                dot_nt(right[t, 0, :, :dim], w[0])
                + dot_nt(right[t, 0, :, dim:], w[1])
                + dot_nt(right[t, 1, :, :dim], w[2])
            )

        @pl.when(jnp.logical_not(is_att))
        def _():
            dmix[...] = dot_nt(right[t, 0, :, :dim], w[0]) + dot_nt(right[t, 0, :, dim:], w[1])

        dn = dmix[...]
        unit = y1[t].astype(f32) * scale
        dgain[...] += jnp.sum(dn * unit, axis=0, keepdims=True)
        weighted = dn * gain_ref[...]
        du = scale * (weighted - unit * jnp.mean(weighted * unit, axis=-1, keepdims=True))
        c2[cot] = (c1[t].astype(f32) + du).astype(bf16)
        hand(c2.at[cot], c2, t + 1, 3, before).start()

        @pl.when(t < TICKS - 1)
        def _():
            hand(y1.at[made], y2, t + 2, 1, before2).start()
            hand(c2.at[cot], c1, t + 2, 2, before2).start()

        return carry

    lax.fori_loop(0, TICKS, tick_body, 0)

    total = dgain[...].astype(bf16).astype(f32)
    for q in range(replicas):
        dgain_send[q] = jnp.broadcast_to(total[:, q * own : (q + 1) * own], dgain_send.shape[1:])

    def gain_copy(j):
        return pltpu.make_async_remote_copy(
            src_ref=dgain_send.at[peers[j]], dst_ref=dgain_all.at[r],
            send_sem=dg_send.at[j], recv_sem=dg_recv.at[j],
            device_id=(s, peers[j]), device_id_type=MESH,
        )

    for j in range(replicas - 1):
        gain_copy(j).start()
    dgain_all[r] = dgain_send[r]

    def share_wait(tick):
        for kind in (0, 2, 1):
            own_copy(tick, kind).wait()
            for j in reversed(range(replicas - 1)):
                share(tick, j, kind).wait()

    tokens = replicas * rows
    chunk = 256

    def accumulate(first, count, fresh):
        span = pl.ds(first * tokens, count * tokens)

        def strip(i, carry):
            cols = pl.ds(pl.multiple_of(i * chunk, chunk), chunk)
            use_normed = jnp.logical_or(core == 0, jnp.logical_and(is_att, i < dim // chunk))

            @pl.when(use_normed)
            def _():
                value = dot_tn(normed_all[span], right_all[span, cols])
                acc[:, cols] = value if fresh else acc[:, cols] + value

            @pl.when(jnp.logical_not(use_normed))
            def _():
                value = dot_tn(second_all[span], right_all[span, cols])
                acc[:, cols] = value if fresh else acc[:, cols] + value

            return carry

        lax.fori_loop(0, wide // chunk, strip, 0)

    for tick in range(TICKS - 1):
        share_wait(tick)
    accumulate(0, TICKS - 1, True)
    share_wait(TICKS - 1)
    accumulate(TICKS - 1, 1, False)

    grad_scale = 1.0 / math.sqrt(TICKS * rows * replicas)
    mine = pl.ds(pl.multiple_of(core * own, own), own)
    cols = pl.ds(pl.multiple_of(core * wide, wide), wide)
    other = CORES - 1 - core
    done[...] = (acc[pl.ds(pl.multiple_of(other * own, own), own), :] * grad_scale).astype(bf16)
    final = pltpu.make_async_remote_copy(
        src_ref=done, dst_ref=grads.at[:, cols],
        send_sem=fin_send, recv_sem=fin_recv,
        device_id=(s, chip * CORES + other), device_id_type=MESH,
    )
    final.start()
    grads[:, cols] = (acc[mine, :] * grad_scale).astype(bf16)

    for j in range(replicas - 1):
        gain_copy(j).wait()
    gain_sum = dgain_all[0, :1]
    for q in range(1, replicas):
        gain_sum = gain_sum + dgain_all[q, :1]
    gain_grads[...] = gain_sum * grad_scale

    hand(y1.at[0], y1, TICKS, 0, before).wait_recv()
    hand(c2.at[0], c2, TICKS, 3, before).wait_recv()
    hand(y2.at[0], y2, TICKS, 1, before).wait_recv()
    hand(c1.at[0], c1, TICKS, 2, before).wait_recv()
    out_streams[0] = y1[TICKS]
    out_streams[1] = y2[TICKS]
    out_cotangents[0] = c1[TICKS]
    out_cotangents[1] = c2[TICKS]
    for slot in range(1, TICKS + 1):
        hand(y1.at[0], y1, slot, 0, before).wait_send()
        hand(c2.at[0], c2, slot, 3, before).wait_send()
        hand(y1.at[0], y2, slot, 1, before).wait_send()
        hand(c2.at[0], c1, slot, 2, before).wait_send()
    final.wait()


def shards(streams, cotangents, weights, norm_gains, segment_ids):
    sections = lax.axis_size("section")
    replicas = lax.axis_size("dp")
    chips = replicas // CORES
    rows, dim = streams.shape[3:]
    full = weights.shape[2]
    wide = full // CORES
    part = dim // chips
    own = dim // replicas
    tokens = TICKS * replicas * rows
    dma = pltpu.SemaphoreType.DMA
    vmem = pl.BlockSpec(memory_space=pltpu.VMEM)
    hbm = pl.BlockSpec(memory_space=pl.ANY)
    flops = 2 * TICKS * rows * dim * full * 3
    out_streams, out_cotangents, grads, gains = pl.pallas_call(
        partial(kernel, sections, replicas),
        out_shape=(
            jax.ShapeDtypeStruct((2, rows, dim), bf16),
            jax.ShapeDtypeStruct((2, rows, dim), bf16),
            jax.ShapeDtypeStruct((own, full), bf16),
            jax.ShapeDtypeStruct((1, own), f32),
        ),
        in_specs=[hbm, hbm, hbm, vmem, vmem],
        out_specs=(vmem, vmem, vmem, vmem),
        scratch_shapes=[
            pltpu.VMEM((4, dim, dim), bf16),
            pltpu.VMEM((2 * TICKS + 1, rows, dim), bf16),
            pltpu.VMEM((TICKS + 1, rows, dim), bf16),
            pltpu.VMEM((TICKS + 1, rows, dim), bf16),
            pltpu.VMEM((2 * TICKS + 1, rows, dim), bf16),
            pltpu.VMEM((rows, 3 * dim), f32),
            pltpu.VMEM((rows, dim), f32),
            pltpu.VMEM((TICKS, CORES, rows, wide), bf16),
            pltpu.VMEM((TICKS, chips, rows, part), bf16),
            pltpu.VMEM((TICKS, chips, rows, part), bf16),
            pltpu.VMEM((tokens, wide), bf16),
            pltpu.VMEM((tokens, part), bf16),
            pltpu.VMEM((tokens, part), bf16),
            pltpu.VMEM((1, dim), f32),
            pltpu.VMEM((replicas, 8, own), f32),
            pltpu.VMEM((replicas, 8, own), f32),
            pltpu.VMEM((part, wide), f32),
            pltpu.VMEM((own, wide), bf16),
            dma((4,)),
            dma((4,)),
            dma((4, TICKS + 1)),
            dma((4, TICKS + 1)),
            dma((3, TICKS)),
            dma((3, TICKS, replicas - 1)),
            dma((3, TICKS, replicas - 1)),
            dma((replicas - 1,)),
            dma((replicas - 1,)),
            dma,
            dma,
        ],
        compiler_params=pltpu.CompilerParams(
            collective_id=0, has_side_effects=True, vmem_limit_bytes=56 * 1024 * 1024
        ),
        cost_estimate=pl.CostEstimate(
            flops=flops, bytes_accessed=2 * dim * full, transcendentals=0
        ),
        name="ticks",
    )(
        streams[:, 0, 0],
        cotangents[:, 0, 0],
        weights[0],
        norm_gains,
        segment_ids,
    )
    return (
        out_streams[:, None, None],
        out_cotangents[:, None, None],
        grads[None],
        gains,
    )


def solution(mesh):
    placed = (
        P(None, "section", "dp", None, None),
        P(None, "section", "dp", None, None),
        P("section", None, None),
        P("section", None),
        P(None, "dp", None),
    )
    return jax.shard_map(
        shards,
        mesh=mesh,
        in_specs=placed,
        out_specs=(
            P(None, "section", "dp", None, None),
            P(None, "section", "dp", None, None),
            P("section", "dp", None),
            P("section", "dp"),
        ),
        check_vma=False,
    )
```

profile of v0, /device:TPU:0, one launch (start us, length us, event | category | flops | bytes accessed | tf_op | source)
XLA Modules:
  0.0 126.1 jit_solution(339383113662244134)
XLA Ops:
  0.6 119.6 %ticks.1 = (bf16[2,128,1024]{2,1,0:T(8,128)(2,1)}, bf16[2,128,1024]{2,1,0:T(8,128)(2,1)}, bf16[256,4096]{1,0:T(8,128)(2,1)}, f32[1,256]{1,0:T(1,128)}) custom-call(bf16[2,128,1024]{2,1,0:T(8,128)(2,1)} %bitcast.14, bf16[2,128,1024]{2,1,0:T(8,128)(2,1)} %bitcast.15, bf16[1024,4096]{1,0:T(8,128)(2,1)} %bitcast.13, f32[1,1024]{1,0:T(1,128)} %gain_ref.1, ...), custom_call_target="tpu_custom_call" | custom-call | flops 9663676416 | bytes 8388608 | tf_op jit(solution)/shard_map/ticks/pallas_call | solution.py:385
  120.3 0.0 copy-start
  120.3 2.0 %copy.15 = bf16[2,1,1,128,1024]{4,3,2,1,0:T(8,128)(2,1)} copy(bf16[2,1,1,128,1024]{4,3,2,1,0:T(8,128)(2,1)} %bitcast.12) | data formatting | bytes 1048576
  122.3 1.9 %copy.16 = bf16[2,1,1,128,1024]{4,3,2,1,0:T(8,128)(2,1)} copy(bf16[2,1,1,128,1024]{4,3,2,1,0:T(8,128)(2,1)} %bitcast.11) | data formatting | bytes 1048576
  124.2 0.0 copy-done
  124.2 0.0 copy-start.1
  124.2 1.3 %copy.17 = bf16[1,256,4096]{2,1,0:T(8,128)(2,1)} copy(bf16[1,256,4096]{2,1,0:T(8,128)(2,1)S(1)} %bitcast.10) | data formatting | bytes 4194304
  125.5 0.0 copy-done.1
  125.5 0.6 copy.18
Async XLA Ops:
  120.3 3.9 %copy-start = (bf16[256,4096]{1,0:T(8,128)(2,1)S(1)}, bf16[256,4096]{1,0:T(8,128)(2,1)}, u32[]{:S(2)}) copy-start(bf16[256,4096]{1,0:T(8,128)(2,1)} %get-tuple-element.10) | copy-start | bytes 6291460
  124.2 1.3 %copy-start.1 = (f32[1,256]{1,0:T(1,128)S(1)}, f32[1,256]{1,0:T(1,128)}, u32[]{:S(2)}) copy-start(f32[1,256]{1,0:T(1,128)} %get-tuple-element.23) | copy-start | bytes 3076
where the time goes:
time: 126 us
  Pallas kernels  120 us (95%)
  local copies, waits for them, and re-layouts  5.77 us (5%)
    pallas_call x1, Pallas kernels, shards(): pl.pallas_call(partial(kernel, sections, replicas), out_shape=(jax.ShapeD...  120 us
    unnamed x8, local copies, waits for them, and re-layouts  5.77 us

commit v1 on v0

--- a/solution.py
+++ b/solution.py
@@ -39,7 +39,7 @@
     w, y1, y2, c1, c2, proj, dmix,
     right, normed, second, right_all, normed_all, second_all,
     dgain, dgain_send, dgain_all, acc, done,
-    w_sem, in_sem, send_sem, recv_sem, own_sem, dp_send, dp_recv, dg_send, dg_recv, fin_send, fin_recv,
+    w_sem, in_sem, send_sem, recv_sem, own_sem, dp_send, dp_recv, fwd_send, fwd_recv, dg_send, dg_recv, fin_send, fin_recv,
 ):
     s = lax.axis_index("section")
     r = lax.axis_index("dp")
@@ -102,16 +102,30 @@
         peer = peers[j]
         peer_core = lax.rem(peer, CORES)
         peer_chip = peer // CORES
+        rows_here = rows_of(tick, r)
         if kind == 0:
-            src, dst = normed.at[tick, peer_chip], normed_all
+            src, dst = normed.at[tick, peer_chip], normed_all.at[rows_here]
         elif kind == 1:
-            src, dst = second.at[tick, peer_chip], second_all
+            src, dst = second.at[tick, peer_chip], second_all.at[rows_here]
         else:
-            src, dst = right.at[tick, peer_core], right_all
+            cols = pl.ds((kind - 2) * dim, dim)
+            src, dst = right.at[tick, peer_core, :, cols], right_all.at[rows_here, cols]
         return pltpu.make_async_remote_copy(
-            src_ref=src, dst_ref=dst.at[rows_of(tick, r)],
+            src_ref=src, dst_ref=dst,
             send_sem=dp_send.at[kind, tick, j], recv_sem=dp_recv.at[kind, tick, j],
             device_id=(s, peer), device_id_type=MESH,
+        )
+
+    partner = chip * CORES + CORES - 1 - core
+    offsets = [CORES * q for q in range(1, chips)]
+
+    def forward(tick, q):
+        source = lax.rem(r + replicas - offsets[q], replicas)
+        span = rows_of(tick, source)
+        return pltpu.make_async_remote_copy(
+            src_ref=normed_all.at[span], dst_ref=normed_all.at[span],
+            send_sem=fwd_send.at[tick, q], recv_sem=fwd_recv.at[tick, q],
+            device_id=(s, partner), device_id_type=MESH,
         )
 
     def own_copy(tick, kind):
@@ -123,10 +137,34 @@
             src, dst = right.at[tick, core], right_all
         return pltpu.make_async_copy(src, dst.at[rows_of(tick, r)], own_sem.at[kind, tick])
 
-    def share_start(tick, kind):
+    def wanted(j):
+        return lax.rem(peers[j], CORES) == CORES - 1
+
+    def near(j):
+        return peers[j] == partner
+
+    def norm_start(tick):
         for j in reversed(range(replicas - 1)):
-            share(tick, j, kind).start()
-        own_copy(tick, kind).start()
+            if j + 1 in offsets:
+                share(tick, j, 0).start()
+            else:
+                @pl.when(near(j))
+                def _(j=j):
+                    share(tick, j, 0).start()
+        own_copy(tick, 0).start()
+
+    def second_start(tick):
+        for j in reversed(range(replicas - 1)):
+            @pl.when(wanted(j))
+            def _(j=j):
+                share(tick, j, 1).start()
+        own_copy(tick, 1).start()
+
+    def right_start(tick, kind, last_core):
+        for j in reversed(range(replicas - 1)):
+            @pl.when(wanted(j) if last_core else jnp.logical_not(wanted(j)))
+            def _(j=j):
+                share(tick, j, kind).start()
 
     def tick_body(t, carry):
         @pl.when(t > 0)
@@ -138,7 +176,7 @@
         n = (stream * scale * gain_ref[...]).astype(bf16)
         for c in range(chips):
             normed[t, c] = n[:, c * part : (c + 1) * part]
-        share_start(t, 0)
+        norm_start(t)
 
         @pl.when(t > 0)
         def _():
@@ -148,10 +186,11 @@
 
         @pl.when(is_att)
         def _():
+            right[t, 1, :, dim:] = c2[t]
+            right_start(t, 3, True)
             for j in range(3):
                 proj[:, j * dim : (j + 1) * dim] = dot_nn(n, w[j])
             dmix[...] = dot_nt(c2[t], w[3])
-            right[t, 1, :, dim:] = c2[t]
             seg = segs[lax.rem(s + t, sections)].astype(f32)
             across = jnp.broadcast_to(seg, (rows, rows))
             row_id = lax.broadcasted_iota(jnp.int32, (rows, rows), 0)
@@ -209,12 +248,17 @@
                 right[t, 1, :, at[0]] = dv.astype(bf16)
                 return carry
 
-            lax.fori_loop(0, HEADS // 2, pair, 0, unroll=2)
+            lax.fori_loop(0, HEADS // 2, pair, 0, unroll=4)
+            right_start(t, 2, False)
+            right_start(t, 3, False)
+            right_start(t, 2, True)
+            second_start(t)
 
         @pl.when(jnp.logical_not(is_att))
         def _():
             for c in range(chips):
                 second[t, c] = c2[t, :, c * part : (c + 1) * part]
+            second_start(t)
             for j in range(2):
                 at = pl.ds(j * dim, dim)
                 proj[:, at] = dot_nn(n, w[j])
@@ -233,9 +277,10 @@
                     return carry
 
                 lax.fori_loop(0, dim // 256, strip, 0)
-
-        share_start(t, 2)
-        share_start(t, 1)
+                right_start(t, 2 + j, False)
+                right_start(t, 2 + j, True)
+
+        own_copy(t, 2).start()
 
         @pl.when(is_att)
         def _():
@@ -277,6 +322,9 @@
             hand(y1.at[made], y2, t + 2, 1, before2).start()
             hand(c2.at[cot], c1, t + 2, 2, before2).start()
 
+        for q in range(chips - 1):
+            share(t, offsets[q] - 1, 0).wait_recv()
+            forward(t, q).start()
         return carry
 
     lax.fori_loop(0, TICKS, tick_body, 0)
@@ -299,8 +347,29 @@
     def share_wait(tick):
         for kind in (0, 2, 1):
             own_copy(tick, kind).wait()
-            for j in reversed(range(replicas - 1)):
-                share(tick, j, kind).wait()
+        for q in range(chips - 1):
+            share(tick, offsets[q] - 1, 0).wait_send()
+            forward(tick, q).wait()
+        for j in reversed(range(replicas - 1)):
+            if j + 1 not in offsets:
+                @pl.when(near(j))
+                def _(j=j):
+                    share(tick, j, 0).wait_send()
+
+                @pl.when(lax.rem(r + replicas - j - 1, replicas) == partner)
+                def _(j=j):
+                    share(tick, j, 0).wait_recv()
+
+            @pl.when(wanted(j))
+            def _(j=j):
+                share(tick, j, 1).wait_send()
+
+            @pl.when(core == CORES - 1)
+            def _(j=j):
+                share(tick, j, 1).wait_recv()
+
+            share(tick, j, 3).wait()
+            share(tick, j, 2).wait()
 
     tokens = replicas * rows
     chunk = 256
@@ -416,8 +485,10 @@
             dma((4, TICKS + 1)),
             dma((4, TICKS + 1)),
             dma((3, TICKS)),
-            dma((3, TICKS, replicas - 1)),
-            dma((3, TICKS, replicas - 1)),
+            dma((4, TICKS, replicas - 1)),
+            dma((4, TICKS, replicas - 1)),
+            dma((TICKS, chips - 1)),
+            dma((TICKS, chips - 1)),
             dma((replicas - 1,)),
             dma((replicas - 1,)),
             dma,

time: 126 us -> 108 us (0.86)
  Pallas kernels: 120 us -> 101 us
    pallas_call x1, Pallas kernels: 120 us -> 101 us  [shards(): pl.pallas_call(partial(kernel, sections, replicas), out_shape=(jax.ShapeD...]
where the time goes in v1:
time: 108 us
  Pallas kernels  101 us (94%)
  local copies, waits for them, and re-layouts  5.77 us (5%)
    pallas_call x1, Pallas kernels, shards(): pl.pallas_call(partial(kernel, sections, replicas), out_shape=(jax.ShapeD...  101 us
    unnamed x8, local copies, waits for them, and re-layouts  5.77 us

profile of v1, /device:TPU:0, one launch (start us, length us, event | category | flops | bytes accessed | tf_op | source)
XLA Modules:
  0.0 107.7 jit_solution(1206251812826373996)
XLA Ops:
  0.6 101.2 %ticks.1 = (bf16[2,128,1024]{2,1,0:T(8,128)(2,1)}, bf16[2,128,1024]{2,1,0:T(8,128)(2,1)}, bf16[256,4096]{1,0:T(8,128)(2,1)}, f32[1,256]{1,0:T(1,128)}) custom-call(bf16[2,128,1024]{2,1,0:T(8,128)(2,1)} %bitcast.14, bf16[2,128,1024]{2,1,0:T(8,128)(2,1)} %bitcast.15, bf16[1024,4096]{1,0:T(8,128)(2,1)} %bitcast.13, f32[1,1024]{1,0:T(1,128)} %gain_ref.1, ...), custom_call_target="tpu_custom_call" | custom-call | flops 9663676416 | bytes 8388608 | tf_op jit(solution)/shard_map/ticks/pallas_call | solution.py:454
  101.9 0.0 copy-start
  101.9 2.0 %copy.15 = bf16[2,1,1,128,1024]{4,3,2,1,0:T(8,128)(2,1)} copy(bf16[2,1,1,128,1024]{4,3,2,1,0:T(8,128)(2,1)} %bitcast.12) | data formatting | bytes 1048576
  103.9 1.9 %copy.16 = bf16[2,1,1,128,1024]{4,3,2,1,0:T(8,128)(2,1)} copy(bf16[2,1,1,128,1024]{4,3,2,1,0:T(8,128)(2,1)} %bitcast.11) | data formatting | bytes 1048576
  105.8 0.0 copy-done
  105.8 0.0 copy-start.1
  105.8 1.3 %copy.17 = bf16[1,256,4096]{2,1,0:T(8,128)(2,1)} copy(bf16[1,256,4096]{2,1,0:T(8,128)(2,1)S(1)} %bitcast.10) | data formatting | bytes 4194304
  107.1 0.0 copy-done.1
  107.1 0.6 copy.18
Async XLA Ops:
  101.9 3.9 %copy-start = (bf16[256,4096]{1,0:T(8,128)(2,1)S(1)}, bf16[256,4096]{1,0:T(8,128)(2,1)}, u32[]{:S(2)}) copy-start(bf16[256,4096]{1,0:T(8,128)(2,1)} %get-tuple-element.10) | copy-start | bytes 6291460
  105.8 1.3 %copy-start.1 = (f32[1,256]{1,0:T(1,128)S(1)}, f32[1,256]{1,0:T(1,128)}, u32[]{:S(2)}) copy-start(f32[1,256]{1,0:T(1,128)} %get-tuple-element.23) | copy-start | bytes 3076

commit v2 on v1

--- a/solution.py
+++ b/solution.py
@@ -91,8 +91,6 @@
 
     hand(y1.at[0], y2, 1, 1, before).start()
     hand(c2.at[0], c1, 1, 2, before).start()
-    for copy in w_loads:
-        copy.wait()
     dgain[...] = jnp.zeros_like(dgain)
 
     def rows_of(tick, replica):
@@ -166,6 +164,12 @@
             def _(j=j):
                 share(tick, j, kind).start()
 
+    def weights_here(t):
+        @pl.when(t == 0)
+        def _():
+            for copy in w_loads:
+                copy.wait()
+
     def tick_body(t, carry):
         @pl.when(t > 0)
         def _():
@@ -188,6 +192,7 @@
         def _():
             right[t, 1, :, dim:] = c2[t]
             right_start(t, 3, True)
+            weights_here(t)
             for j in range(3):
                 proj[:, j * dim : (j + 1) * dim] = dot_nn(n, w[j])
             dmix[...] = dot_nt(c2[t], w[3])
@@ -259,6 +264,7 @@
             for c in range(chips):
                 second[t, c] = c2[t, :, c * part : (c + 1) * part]
             second_start(t)
+            weights_here(t)
             for j in range(2):
                 at = pl.ds(j * dim, dim)
                 proj[:, at] = dot_nn(n, w[j])
@@ -345,7 +351,7 @@
     dgain_all[r] = dgain_send[r]
 
     def share_wait(tick):
-        for kind in (0, 2, 1):
+        for kind in (0, 2):
             own_copy(tick, kind).wait()
         for q in range(chips - 1):
             share(tick, offsets[q] - 1, 0).wait_send()
@@ -360,6 +366,9 @@
                 def _(j=j):
                     share(tick, j, 0).wait_recv()
 
+    def second_wait(tick):
+        own_copy(tick, 1).wait()
+        for j in reversed(range(replicas - 1)):
             @pl.when(wanted(j))
             def _(j=j):
                 share(tick, j, 1).wait_send()
@@ -368,13 +377,18 @@
             def _(j=j):
                 share(tick, j, 1).wait_recv()
 
-            share(tick, j, 3).wait()
-            share(tick, j, 2).wait()
+    def piece_wait(tick, piece):
+        for j in reversed(range(replicas - 1)):
+            share(tick, j, 2 + piece).wait()
+
+        @pl.when(is_att if piece == 1 else jnp.logical_not(is_att))
+        def _():
+            second_wait(tick)
 
     tokens = replicas * rows
     chunk = 256
 
-    def accumulate(first, count, fresh):
+    def accumulate(first, count, fresh, low, high):
         span = pl.ds(first * tokens, count * tokens)
 
         def strip(i, carry):
@@ -393,33 +407,43 @@
 
             return carry
 
-        lax.fori_loop(0, wide // chunk, strip, 0)
+        lax.fori_loop(low // chunk, high // chunk, strip, 0)
 
     for tick in range(TICKS - 1):
         share_wait(tick)
-    accumulate(0, TICKS - 1, True)
-    share_wait(TICKS - 1)
-    accumulate(TICKS - 1, 1, False)
-
-    grad_scale = 1.0 / math.sqrt(TICKS * rows * replicas)
-    mine = pl.ds(pl.multiple_of(core * own, own), own)
-    cols = pl.ds(pl.multiple_of(core * wide, wide), wide)
-    other = CORES - 1 - core
-    done[...] = (acc[pl.ds(pl.multiple_of(other * own, own), own), :] * grad_scale).astype(bf16)
-    final = pltpu.make_async_remote_copy(
-        src_ref=done, dst_ref=grads.at[:, cols],
-        send_sem=fin_send, recv_sem=fin_recv,
-        device_id=(s, chip * CORES + other), device_id_type=MESH,
-    )
-    final.start()
-    grads[:, cols] = (acc[mine, :] * grad_scale).astype(bf16)
+        for piece in range(2):
+            piece_wait(tick, piece)
+    accumulate(0, TICKS - 1, True, 0, wide)
 
     for j in range(replicas - 1):
         gain_copy(j).wait()
     gain_sum = dgain_all[0, :1]
     for q in range(1, replicas):
         gain_sum = gain_sum + dgain_all[q, :1]
+    grad_scale = 1.0 / math.sqrt(TICKS * rows * replicas)
     gain_grads[...] = gain_sum * grad_scale
+
+    mine = pl.ds(pl.multiple_of(core * own, own), own)
+    other = CORES - 1 - core
+    theirs = pl.ds(pl.multiple_of(other * own, own), own)
+
+    def final(piece):
+        cols = pl.ds(pl.multiple_of(core * wide + piece * dim, dim), dim)
+        return pltpu.make_async_remote_copy(
+            src_ref=done.at[:, pl.ds(piece * dim, dim)], dst_ref=grads.at[:, cols],
+            send_sem=fin_send.at[piece], recv_sem=fin_recv.at[piece],
+            device_id=(s, partner), device_id_type=MESH,
+        )
+
+    share_wait(TICKS - 1)
+    for piece in range(2):
+        piece_wait(TICKS - 1, piece)
+        accumulate(TICKS - 1, 1, False, piece * dim, (piece + 1) * dim)
+        here = pl.ds(piece * dim, dim)
+        done[:, here] = (acc[theirs, here] * grad_scale).astype(bf16)
+        final(piece).start()
+        cols = pl.ds(pl.multiple_of(core * wide + piece * dim, dim), dim)
+        grads[:, cols] = (acc[mine, here] * grad_scale).astype(bf16)
 
     hand(y1.at[0], y1, TICKS, 0, before).wait_recv()
     hand(c2.at[0], c2, TICKS, 3, before).wait_recv()
@@ -434,7 +458,8 @@
         hand(c2.at[0], c2, slot, 3, before).wait_send()
         hand(y1.at[0], y2, slot, 1, before).wait_send()
         hand(c2.at[0], c1, slot, 2, before).wait_send()
-    final.wait()
+    for piece in range(2):
+        final(piece).wait()
 
 
 def shards(streams, cotangents, weights, norm_gains, segment_ids):
@@ -491,8 +516,8 @@
             dma((TICKS, chips - 1)),
             dma((replicas - 1,)),
             dma((replicas - 1,)),
-            dma,
-            dma,
+            dma((2,)),
+            dma((2,)),
         ],
         compiler_params=pltpu.CompilerParams(
             collective_id=0, has_side_effects=True, vmem_limit_bytes=56 * 1024 * 1024

time: 108 us -> 108 us (level)
  no operation moved by 1% of the time
where the time goes in v2:
time: 108 us; the launch traced here: 107 us
  Pallas kernels  101 us (94%)
  local copies, waits for them, and re-layouts  5.77 us (5%)
    pallas_call x1, Pallas kernels, shards(): pl.pallas_call(partial(kernel, sections, replicas), out_shape=(jax.ShapeD...  101 us
    unnamed x8, local copies, waits for them, and re-layouts  5.77 us

profile of v2, /device:TPU:0, one launch (start us, length us, event | category | flops | bytes accessed | tf_op | source)
XLA Modules:
  0.0 107.4 jit_solution(11328652778011504740)
XLA Ops:
  0.6 101.0 %ticks.1 = (bf16[2,128,1024]{2,1,0:T(8,128)(2,1)}, bf16[2,128,1024]{2,1,0:T(8,128)(2,1)}, bf16[256,4096]{1,0:T(8,128)(2,1)}, f32[1,256]{1,0:T(1,128)}) custom-call(bf16[2,128,1024]{2,1,0:T(8,128)(2,1)} %bitcast.14, bf16[2,128,1024]{2,1,0:T(8,128)(2,1)} %bitcast.15, bf16[1024,4096]{1,0:T(8,128)(2,1)} %bitcast.13, f32[1,1024]{1,0:T(1,128)} %gain_ref.1, ...), custom_call_target="tpu_custom_call" | custom-call | flops 9663676416 | bytes 8388608 | tf_op jit(solution)/shard_map/ticks/pallas_call | solution.py:479
  101.6 0.0 copy-start
  101.7 2.0 %copy.15 = bf16[2,1,1,128,1024]{4,3,2,1,0:T(8,128)(2,1)} copy(bf16[2,1,1,128,1024]{4,3,2,1,0:T(8,128)(2,1)} %bitcast.12) | data formatting | bytes 1048576
  103.7 1.9 %copy.16 = bf16[2,1,1,128,1024]{4,3,2,1,0:T(8,128)(2,1)} copy(bf16[2,1,1,128,1024]{4,3,2,1,0:T(8,128)(2,1)} %bitcast.11) | data formatting | bytes 1048576
  105.5 0.0 copy-done
  105.5 0.0 copy-start.1
  105.5 1.3 %copy.17 = bf16[1,256,4096]{2,1,0:T(8,128)(2,1)} copy(bf16[1,256,4096]{2,1,0:T(8,128)(2,1)S(1)} %bitcast.10) | data formatting | bytes 4194304
  106.9 0.0 copy-done.1
  106.9 0.6 copy.18
Async XLA Ops:
  101.6 3.9 %copy-start = (bf16[256,4096]{1,0:T(8,128)(2,1)S(1)}, bf16[256,4096]{1,0:T(8,128)(2,1)}, u32[]{:S(2)}) copy-start(bf16[256,4096]{1,0:T(8,128)(2,1)} %get-tuple-element.10) | copy-start | bytes 6291460
  105.5 1.3 %copy-start.1 = (f32[1,256]{1,0:T(1,128)S(1)}, f32[1,256]{1,0:T(1,128)}, u32[]{:S(2)}) copy-start(f32[1,256]{1,0:T(1,128)} %get-tuple-element.23) | copy-start | bytes 3076
